TPU v7x, 512 devices: a whole 4x4x16 slice. The times are simulated.
512 devices in a mesh: row: 32 (over z, core), col: 16 (over x, y).
Axes of the slice: x: 4, y: 4, z: 16, core: 2. Of those that a mesh axis runs over, the one named last changes fastest.
Arguments:
- currents: float32 [96, 8192], P(None, ('row', 'col')), may hold values from -6 to 6
- residual: float32 [96, 8192], P(None, ('row', 'col')), may hold values from -6 to 6
- shadow: float32 [96, 8192], P(None, ('row', 'col')), may hold values from -6 to 6
- lattice_sites: int32 [3, 8192], P(None, ('row', 'col')), may hold values from 0 to 127, as said below
- classes: int32 [8192], P(('row', 'col')), may hold values from 0 to 3
- inverse_polarizability: float32 [2, 4], replicated, may hold values from 2 to 6
Outputs:
- image: float32 [96, 8192], P(None, ('row', 'col'))
- half_step: float32 [96, 8192], P(None, ('row', 'col'))
Inputs may be any that keep to these rules, and one draw needn't show every extreme that they name: `lattice_sites`: every site of the lattice with x below 32, y below 128 and z 0 or 1 holds exactly one dipole; no two dipoles share a site.
All inputs are finite; a program needn't handle non-finite values.
Results may differ from a plain program's by a relative error of at most 0.0003.
Values sent between devices are 32-bit elements; how exact they have to be, the bound alone decides.
A program may use at most 64 MiB of HBM per device.

v0:
```python
import math

import jax
import jax.numpy as jnp
from jax import lax
from jax.sharding import PartitionSpec as P

SH = 16


wavenumber = 0.9


def green_apply(target_sites, source_sites, source_flows):
    separation = target_sites[:, :, None] - source_sites[:, None, :]
    distance_sq = jnp.sum(separation * separation, axis=0)
    present = distance_sq > 0.5
    distance = jnp.sqrt(jnp.where(present, distance_sq, 1.0))
    inverse = 1.0 / distance
    unit_dir = separation * inverse
    phase_cos = jnp.cos(wavenumber * distance)
    phase_sin = jnp.sin(wavenumber * distance)
    reach = jnp.where(present, inverse, 0.0)
    iso_real = wavenumber * wavenumber - inverse * inverse
    iso_imag = wavenumber * inverse
    dyad_real = 3.0 * inverse * inverse - wavenumber * wavenumber
    dyad_imag = -3.0 * wavenumber * inverse
    iso_re = (phase_cos * iso_real - phase_sin * iso_imag) * reach
    iso_im = (phase_sin * iso_real + phase_cos * iso_imag) * reach
    dyad_re = (phase_cos * dyad_real - phase_sin * dyad_imag) * reach
    dyad_im = (phase_sin * dyad_real + phase_cos * dyad_imag) * reach
    identity = jnp.eye(3, dtype=jnp.float32)[:, :, None, None]
    outer = unit_dir[:, None] * unit_dir[None, :]
    tensor_re = identity * iso_re + outer * dyad_re
    tensor_im = identity * iso_im + outer * dyad_im
    flows = source_flows.reshape(2, 3, -1, source_flows.shape[1])
    real_part = jnp.einsum("cdts,bdks->bckt", tensor_re, flows, precision=lax.Precision.HIGHEST)
    imag_part = jnp.einsum("cdts,bdks->bckt", tensor_im, flows, precision=lax.Precision.HIGHEST)
    field = jnp.stack([real_part[0] - imag_part[1], real_part[1] + imag_part[0]])
    return field.reshape(source_flows.shape[0], target_sites.shape[1])


def make_folder(targets, running, pieces):
    flows, spots = pieces
    planes = flows.shape[0]
    shard_groups = flows.shape[1] // SH
    wanted = max(1, 32768 // (targets.shape[1] * SH))
    grouping = math.gcd(shard_groups, wanted)
    block_width = grouping * SH
    block_count = shard_groups // grouping
    flow_blocks = flows.reshape(planes, block_count, block_width).transpose(1, 0, 2)
    spot_blocks = spots.reshape(3, block_count, block_width).transpose(1, 0, 2)

    def advance(accumulated, item_pair):
        return (accumulated + green_apply(targets, item_pair[1], item_pair[0]), None)

    accumulated, unused = lax.scan(advance, running, (flow_blocks, spot_blocks))
    return accumulated


def paired(shadow4, other_re, other_im):
    real_sum = jnp.sum(shadow4[0] * other_re + shadow4[1] * other_im, axis=(0, 2))
    imag_sum = jnp.sum(shadow4[0] * other_im - shadow4[1] * other_re, axis=(0, 2))
    return (real_sum, imag_sum)


def local(currents, residual, shadow, lattice_sites, classes, inverse_polarizability):
    planes = currents.shape[0]
    owned = currents.shape[1]
    places = lattice_sites.astype(jnp.float32)
    shadow4 = shadow.reshape(2, 3, -1, owned)
    resid4 = residual.reshape(2, 3, -1, owned)
    rho_re, rho_im = lax.psum(paired(shadow4, resid4[0], resid4[1]), ("row", "col"))
    empty = jnp.zeros((planes, owned), jnp.float32)
    fields = make_folder(
        places,
        empty,
        (
            lax.all_gather(currents, ("row", "col"), axis=1, tiled=True),
            lax.all_gather(places, ("row", "col"), axis=1, tiled=True),
        ),
    )
    flows4 = currents.reshape(2, 3, -1, owned)
    fields4 = fields.reshape(2, 3, -1, owned)
    onehot = (
        classes[None, :] == jnp.arange(inverse_polarizability.shape[1], dtype=jnp.int32)[:, None]
    ).astype(jnp.float32)
    pol_re = jnp.sum(inverse_polarizability[0][:, None] * onehot, axis=0)
    pol_im = jnp.sum(inverse_polarizability[1][:, None] * onehot, axis=0)
    image_re = pol_re * flows4[0] - pol_im * flows4[1] - fields4[0]
    image_im = pol_re * flows4[1] + pol_im * flows4[0] - fields4[1]
    den_re, den_im = lax.psum(paired(shadow4, image_re, image_im), ("row", "col"))
    magnitude = jnp.maximum(den_re * den_re + den_im * den_im, 1.0)
    alpha_re = ((rho_re * den_re + rho_im * den_im) / magnitude)[None, :, None]
    alpha_im = ((rho_im * den_re - rho_re * den_im) / magnitude)[None, :, None]
    half_re = resid4[0] - (alpha_re * image_re - alpha_im * image_im)
    half_im = resid4[1] - (alpha_re * image_im + alpha_im * image_re)
    image_out = jnp.stack([image_re, image_im]).reshape(planes, owned)
    return (image_out, jnp.stack([half_re, half_im]).reshape(planes, owned))


def solution(mesh):
    in_specs = (
        P(None, ("row", "col")),
        P(None, ("row", "col")),
        P(None, ("row", "col")),
        P(None, ("row", "col")),
        P(("row", "col")),
        P(),
    )
    out_specs = (P(None, ("row", "col")), P(None, ("row", "col")))
    return jax.shard_map(local, mesh=mesh, in_specs=in_specs, out_specs=out_specs, check_vma=False)
```

profile of v0, /device:TPU:1, one launch (start us, length us, event | category | flops | bytes accessed | tf_op | source)
XLA Modules:
  0.0 406.5 jit_solution(4336023659604706390)
XLA Ops:
  7.2 0.7 all-gather.3.cloned.1.call-update
  7.9 0.8 fusion.32
  8.8 0.8 fusion.33
  9.8 0.8 fusion.34
  10.9 0.7 convert_bitcast_fusion
  11.6 240.1 %all-gather = f32[512,16,3]{1,2,0:T(4,128)S(1)} all-gather(f32[1,16,3]{1,2,0:T(4,128)S(1)} %get-tuple-element.150), channel_id=1, replica_groups=mesh['row'=32,'col'=16] {'row','col'}, dimensions={0}, use_global_device_ids=true | all-gather | bytes 98496 | tf_op jit(solution)/shard_map/all_gather | solution.py:80
  252.5 4.0 copy.91
  256.6 38.4 %while.13 = (s32[]{:T(128)}, f32[96,16]{1,0:T(8,128)S(1)}, f32[4,96,2048]{2,0,1:T(4,128)S(1)}, f32[3,16]{1,0:T(4,128)S(1)}, f32[4,3,2048]{2,0,1:T(4,128)S(1)}, /*index=5*/s32[]{:T(128)}, s32[]{:T(128)}) while((s32[]{:T(128)}, f32[96,16]{1,0:T(8,128)S(1)}, f32[4,96,2048]{2,0,1:T(4,128)S(1)}, f32[3,16]{1,0:T(4,128)S(1)}, ...), condition=%wide.region_4.5_spmd.clone, body=%wide.region_2.4_spmd.clone.sunk | while | flops 230234128 | bytes 7680595 | solution.py:57
  256.8 0.6 subtract_multiply_fusion.6
  257.5 0.8 constant_dynamic-slice_fusion.4
  258.6 3.8 fusion.52
  262.4 3.7 fusion.51
  267.1 0.8 constant_dynamic-slice_fusion.4
  268.2 3.7 fusion.52
  272.0 3.7 fusion.51
  276.7 0.8 constant_dynamic-slice_fusion.4
  277.8 3.7 fusion.52
  281.6 3.7 fusion.51
  286.3 0.8 constant_dynamic-slice_fusion.4
  287.4 3.7 fusion.52
  291.2 3.7 fusion.51
  295.6 102.5 %all-reduce = (f32[16]{0:T(128)S(1)}, f32[16]{0:T(128)S(1)}, f32[16]{0:T(128)S(1)}, f32[16]{0:T(128)S(1)}) all-reduce(f32[16]{0:T(128)S(1)} %reduce_sum.98, f32[16]{0:T(128)S(1)} %reduce_sum.107, f32[16]{0:T(128)S(1)} %reduce_sum.104, f32[16]{0:T(128)S(1)} %reduce_sum.101), channel_id=1, replica_groups=mesh['row'=32,'col'=16] {'row','col'}, use_global_device_ids=true, to_apply=%region_7.8 | all-reduce | flops 64 | bytes 512 | tf_op jit(solution)/shard_map/psum | solution.py:73
  398.3 0.7 copy.92
  399.0 0.7 copy.93
  (71 shorter events, 6.0 us)
Async XLA Ops:
  7.2 245.3 %all-gather.3.cloned.1.call-start = ((), (), s32[]{:S(2)}) async-start(), calls=%async_computation | async-start | bytes 4202496 | tf_op jit(solution)/shard_map/all_gather | solution.py:79
  251.7 0.7 copy-start
  251.7 0.7 copy-start.1
Sparse Core Ops, SparseCore 0:
  12.6 203.8 all-gather.2
where the time goes:
time: 407 us; the launch traced here: 406 us
  blocking collectives  343 us (84%)
  matrix products  30 us (7%)
  between operations  14.1 us (3%)
  local copies, waits for them, and re-layouts  13.9 us (3%)
  other arithmetic  4.65 us (1%)
    all_gather x1, blocking collectives, local(): lax.all_gather(places, ('row', 'col'), axis=1, tiled=True)  240 us
    psum x1, blocking collectives, local(): lax.psum(paired(shadow4, resid4[0], resid4[1]), ('row', 'col'))  103 us
    dot_general x4, matrix products, green_apply(): jnp.einsum('cdts,bdks->bckt', tensor_im, flows, precision=lax.Precision.H...  15 us
    dot_general x4, matrix products, green_apply(): jnp.einsum('cdts,bdks->bckt', tensor_re, flows, precision=lax.Precision.H...  15 us
  transfers between devices with their start and end apart: 1, of which 0 were waited for; matrix products, arithmetic and copies ran while one was open for 1% of the time, Pallas kernels for 0%

commit v1 on v0

v1 whole, which is shorter than its diff:
```python
import functools
import math

import jax
import jax.numpy as jnp
import numpy as np
from jax import lax
from jax.experimental import pallas as pl
from jax.experimental.pallas import tpu as pltpu
from jax.sharding import PartitionSpec as P

MESH = pl.DeviceIdType.MESH
K = 0.9
SH = 16
PLANES = 96
PAIRS = ((0, 0), (1, 1), (2, 2), (0, 1), (0, 2), (1, 2))


def _fit(terms, odd):
    nodes = 0.5 * np.cos((np.arange(400) + 0.5) * np.pi / 400)
    powers = np.arange(terms) * 2 + (1 if odd else 0)
    values = np.sin(2 * np.pi * nodes) if odd else np.cos(2 * np.pi * nodes)
    solved = np.linalg.lstsq(nodes[:, None] ** powers[None, :], values, rcond=None)[0]
    return [float(x) for x in solved]


SIN = _fit(6, True)
COS = _fit(7, False)


def _horner(coefs, x):
    out = jnp.float32(coefs[-1])
    for coef in coefs[-2::-1]:
        out = out * x + jnp.float32(coef)
    return out


def green(tx, ty, tz, sx, sy, sz):
    dx, dy, dz = tx - sx, ty - sy, tz - sz
    xx, yy, zz = dx * dx, dy * dy, dz * dz
    dist_sq = xx + yy + zz
    safe = jnp.maximum(dist_sq, 1.0)
    inv = lax.rsqrt(safe)
    dist = safe * inv
    reach = inv * jnp.minimum(dist_sq, 1.0)
    turns = dist * jnp.float32(K / (2 * math.pi))
    frac = turns - jnp.round(turns)
    frac_sq = frac * frac
    e_re = _horner(COS, frac_sq) * reach
    e_im = _horner(SIN, frac_sq) * frac * reach
    inv_sq = inv * inv
    iso_re = jnp.float32(K * K) - inv_sq
    iso_im = jnp.float32(K) * inv
    a_re = e_re * iso_re - e_im * iso_im
    a_im = e_im * iso_re + e_re * iso_im
    b_re = (jnp.float32(2 * K * K) * e_re - 3.0 * a_re) * inv_sq
    b_im = (jnp.float32(2 * K * K) * e_im - 3.0 * a_im) * inv_sq
    outer = (xx, yy, zz, dx * dy, dx * dz, dy * dz)
    parts = []
    for place, product in enumerate(outer):
        re, im = product * b_re, product * b_im
        if place < 3:
            re, im = re + a_re, im + a_im
        parts.extend((re, im))
    return parts


def rows(array, b, component):
    start = b * 48 + component * 16
    return array[start : start + 16]


def dots(left_re, left_im, right_re, right_im):
    return left_re * right_re + left_im * right_im, left_re * right_im - left_im * right_re


def body(
    R, C,
    cur_hbm, res_hbm, sha_hbm, site_hbm, cls_hbm, pol_hbm,
    img_out, half_out,
    cur, res, sha, site, cls, pol,
    stage, src_all, tgt_all, tgt_t, ghi, glo, rs_send, rs_recv, fin_all,
    in_sems, send_sems, recv_sems,
):
    r, c = lax.axis_index("row"), lax.axis_index("col")
    T, S = C * SH, R * SH
    pairs = ((cur_hbm, cur), (res_hbm, res), (sha_hbm, sha), (site_hbm, site), (cls_hbm, cls), (pol_hbm, pol))
    loads = [pltpu.make_async_copy(a, b, in_sems.at[i]) for i, (a, b) in enumerate(pairs)]
    for load in loads:
        load.start()

    barrier = pltpu.get_barrier_semaphore()

    def greet_row(i, carry):
        pl.semaphore_signal(barrier, inc=1, device_id={"row": lax.rem(r + i, R)}, device_id_type=MESH)
        return carry

    def greet_col(i, carry):
        pl.semaphore_signal(barrier, inc=1, device_id={"col": lax.rem(c + i, C)}, device_id_type=MESH)
        return carry

    lax.fori_loop(1, R, greet_row, 0)
    lax.fori_loop(1, C, greet_col, 0)

    stage[...] = jnp.zeros_like(stage)
    for load in loads:
        load.wait()

    stage[0:PLANES, 0:SH] = cur[...]
    stage[PLANES : PLANES + 3, 0:SH] = site[...].astype(jnp.float32)
    src_all[r] = stage[...].T[0:SH]
    stage[0:PLANES, 0:SH] = sha[...]
    tgt_all[c] = stage[...].T[0:SH]
    pl.semaphore_wait(barrier, R + C - 2)

    def send_src(i, carry):
        pltpu.make_async_remote_copy(
            src_ref=src_all.at[r], dst_ref=src_all.at[r], send_sem=send_sems.at[0], recv_sem=recv_sems.at[0],
            device_id={"row": lax.rem(r + i, R)}, device_id_type=MESH,
        ).start()
        return carry

    def send_tgt(i, carry):
        pltpu.make_async_remote_copy(
            src_ref=tgt_all.at[c], dst_ref=tgt_all.at[c], send_sem=send_sems.at[1], recv_sem=recv_sems.at[1],
            device_id={"col": lax.rem(c + i, C)}, device_id_type=MESH,
        ).start()
        return carry

    def drained(buffer, count, which):
        whole = buffer.at[pl.ds(0, count)]
        return pltpu.make_async_remote_copy(
            src_ref=whole, dst_ref=whole, send_sem=send_sems.at[which], recv_sem=recv_sems.at[which],
            device_id={"row": lax.rem(r + 1, R)}, device_id_type=MESH,
        )

    lax.fori_loop(1, C, send_tgt, 0)
    lax.fori_loop(1, R, send_src, 0)

    class_id = cls[...]
    pol_re = jnp.zeros((1, SH), jnp.float32)
    pol_im = jnp.zeros((1, SH), jnp.float32)
    for kind in range(pol.shape[1]):
        pol_re = jnp.where(class_id == kind, pol[0:1, kind : kind + 1], pol_re)
        pol_im = jnp.where(class_id == kind, pol[1:2, kind : kind + 1], pol_im)
    own_re, own_im = [], []
    den_re = den_im = rho_re = rho_im = 0.0
    for comp in range(3):
        cr, ci = rows(cur, 0, comp), rows(cur, 1, comp)
        sr, si = rows(sha, 0, comp), rows(sha, 1, comp)
        own_re.append(pol_re * cr - pol_im * ci)
        own_im.append(pol_re * ci + pol_im * cr)
        re, im = dots(sr, si, own_re[-1], own_im[-1])
        den_re, den_im = den_re + re, den_im + im
        re, im = dots(sr, si, rows(res, 0, comp), rows(res, 1, comp))
        rho_re, rho_im = rho_re + re, rho_im + im
    own_den_re, own_den_im, rho_re, rho_im = (
        jnp.sum(x, axis=1, keepdims=True) for x in (den_re, den_im, rho_re, rho_im)
    )

    drained(tgt_all, C - 1, 1).wait()
    tgt_t[...] = tgt_all[...].reshape(T, 128).T
    tx, ty, tz = (tgt_t[PLANES + i : PLANES + i + 1, :] for i in range(3))
    drained(src_all, R - 1, 0).wait()

    def fill(j, carry):
        block = src_all[j]
        sx, sy, sz = (block[:, PLANES + i : PLANES + i + 1] for i in range(3))
        place = pl.ds(pl.multiple_of(j * SH, SH), SH)
        for which, value in enumerate(green(tx, ty, tz, sx, sy, sz)):
            high = value.astype(jnp.bfloat16)
            ghi[which, place, :] = high
            glo[which, place, :] = (value - high.astype(jnp.float32)).astype(jnp.bfloat16)
        return carry

    lax.fori_loop(0, R, fill, 0)

    flows = src_all[...].reshape(S, 128).T
    f_hi = flows.astype(jnp.bfloat16)
    f_lo = (flows - f_hi.astype(jnp.float32)).astype(jnp.bfloat16)

    def two(array, comp):
        return [rows(array, 0, comp), rows(array, 1, comp)]

    sums = [[0.0, 0.0, 0.0], [0.0, 0.0, 0.0]]
    for which, (a, b) in enumerate(PAIRS):
        high = two(f_hi, a) if a == b else two(f_hi, b) + two(f_hi, a)
        low = two(f_lo, a) if a == b else two(f_lo, b) + two(f_lo, a)
        height = 16 * len(high)
        both = jnp.concatenate(high + low, axis=0)
        high = both[:height]
        for part in range(2):
            one = jnp.dot(both, ghi[2 * which + part], preferred_element_type=jnp.float32)
            other = jnp.dot(high, glo[2 * which + part], preferred_element_type=jnp.float32)
            got = one[:height] + one[height:] + other
            sums[part][a] = sums[part][a] + got[:32]
            if a != b:
                sums[part][b] = sums[part][b] + got[32:]

    field_re = [sums[0][i][:16] - sums[1][i][16:] for i in range(3)]
    field_im = [sums[0][i][16:] + sums[1][i][:16] for i in range(3)]
    den_re = den_im = 0.0
    for comp in range(3):
        re, im = dots(rows(tgt_t, 0, comp), rows(tgt_t, 1, comp), field_re[comp], field_im[comp])
        den_re, den_im = den_re + re, den_im + im
    den_re = own_den_re - jnp.sum(den_re, axis=1, keepdims=True)
    den_im = own_den_im - jnp.sum(den_im, axis=1, keepdims=True)
    early = lax.broadcasted_iota(jnp.int32, (16, T), 1) % 16 < 8
    tail_re = jnp.where(early, den_re, rho_re)
    tail_im = jnp.where(early, den_im, rho_im)
    partial = jnp.concatenate(field_re + field_im + [tail_re, tail_im], axis=0)
    rs_send[...] = partial.T.reshape(C, SH, 128)

    def send_field(i, carry):
        peer = lax.rem(c + i, C)
        pltpu.make_async_remote_copy(
            src_ref=rs_send.at[peer], dst_ref=rs_recv.at[c], send_sem=send_sems.at[2], recv_sem=recv_sems.at[2],
            device_id={"col": peer}, device_id_type=MESH,
        ).start()
        return carry

    lax.fori_loop(1, C, send_field, 0)
    rs_recv[c] = rs_send[c]
    drained(rs_recv, C - 1, 2).wait()
    total = jnp.sum(rs_recv[...], axis=0)
    lane = lax.broadcasted_iota(jnp.int32, (8, 128), 1)
    fin_all[r] = jnp.where(lane >= 96, total[0:8], pltpu.roll(total[8:16], 96, 1))[0:1]

    def send_fin(i, carry):
        pltpu.make_async_remote_copy(
            src_ref=fin_all.at[r], dst_ref=fin_all.at[r], send_sem=send_sems.at[3], recv_sem=recv_sems.at[3],
            device_id={"row": lax.rem(r + i, R)}, device_id_type=MESH,
        ).start()
        return carry

    lax.fori_loop(1, R, send_fin, 0)

    stage[0:SH, :] = total
    field = stage[...].T[:, 0:SH]
    image_re = [own_re[i] - rows(field, 0, i) for i in range(3)]
    image_im = [own_im[i] - rows(field, 1, i) for i in range(3)]
    img_out[...] = jnp.concatenate(image_re + image_im, axis=0)

    drained(fin_all, R - 1, 3).wait()
    ends = jnp.sum(fin_all[...], axis=0)
    lane = lax.broadcasted_iota(jnp.int32, (16, 128), 1)
    angle = lax.broadcasted_iota(jnp.int32, (16, 128), 0)

    def column(start):
        return jnp.sum(jnp.where(lane == angle + start, ends, 0.0), axis=1, keepdims=True)

    rho_re, rho_im, den_re, den_im = column(64), column(80), column(96), column(112)
    magnitude = jnp.maximum(den_re * den_re + den_im * den_im, 1.0)
    alpha_re = (rho_re * den_re + rho_im * den_im) / magnitude
    alpha_im = (rho_im * den_re - rho_re * den_im) / magnitude
    half_re = [rows(res, 0, i) - (alpha_re * image_re[i] - alpha_im * image_im[i]) for i in range(3)]
    half_im = [rows(res, 1, i) - (alpha_re * image_im[i] + alpha_im * image_re[i]) for i in range(3)]
    half_out[...] = jnp.concatenate(half_re + half_im, axis=0)


def local(R, C, currents, residual, shadow, lattice_sites, classes, inverse_polarizability):
    f32 = jnp.float32
    T, S = C * SH, R * SH
    shape = jax.ShapeDtypeStruct((PLANES, SH), f32)
    return pl.pallas_call(
        functools.partial(body, R, C),
        out_shape=(shape, shape),
        in_specs=[pl.BlockSpec(memory_space=pl.ANY)] * 6,
        out_specs=(pl.BlockSpec(memory_space=pltpu.VMEM), pl.BlockSpec(memory_space=pltpu.VMEM)),
        scratch_shapes=[
            pltpu.VMEM((PLANES, SH), f32),
            pltpu.VMEM((PLANES, SH), f32),
            pltpu.VMEM((PLANES, SH), f32),
            pltpu.VMEM((3, SH), jnp.int32),
            pltpu.VMEM((1, SH), jnp.int32),
            pltpu.VMEM(inverse_polarizability.shape, f32),
            pltpu.VMEM((128, 128), f32),
            pltpu.VMEM((R, SH, 128), f32),
            pltpu.VMEM((C, SH, 128), f32),
            pltpu.VMEM((128, T), f32),
            pltpu.VMEM((12, S, T), jnp.bfloat16),
            pltpu.VMEM((12, S, T), jnp.bfloat16),
            pltpu.VMEM((C, SH, 128), f32),
            pltpu.VMEM((C, SH, 128), f32),
            pltpu.VMEM((R, 1, 128), f32),
            pltpu.SemaphoreType.DMA((6,)),
            pltpu.SemaphoreType.DMA((4,)),
            pltpu.SemaphoreType.DMA((4,)),
        ],
        compiler_params=pltpu.CompilerParams(
            collective_id=0, has_side_effects=True, vmem_limit_bytes=32 * 1024 * 1024
        ),
    )(currents, residual, shadow, lattice_sites, classes.reshape(1, SH), inverse_polarizability)


def solution(mesh):
    both = ("row", "col")
    in_specs = (P(None, both), P(None, both), P(None, both), P(None, both), P(both), P())
    out_specs = (P(None, both), P(None, both))
    step = functools.partial(local, mesh.shape["row"], mesh.shape["col"])
    return jax.shard_map(step, mesh=mesh, in_specs=in_specs, out_specs=out_specs, check_vma=False)
```

time: 407 us -> 57.1 us (0.14)
  blocking collectives: 343 us -> 0 us
  Pallas kernels: 0 us -> 52.7 us
  matrix products: 30 us -> 0 us
  between operations: 14.1 us -> 0.66 us
  local copies, waits for them, and re-layouts: 13.9 us -> 3.52 us
  other arithmetic: 4.65 us -> 0 us
    all_gather x1 -> x0, blocking collectives: 240 us -> none  [local(): lax.all_gather(places, ('row', 'col'), axis=1, tiled=True)]
    psum x1 -> x0, blocking collectives: 103 us -> none  [local(): lax.psum(paired(shadow4, resid4[0], resid4[1]), ('row', 'col'))]
    pallas_call x0 -> x1, Pallas kernels: none -> 52.7 us  [local(): pl.pallas_call(functools.partial(body, R, C), out_shape=(shape, shape), i...]
    dot_general x8 -> x0, matrix products: 30 us -> none  [the longest x4 15 us: green_apply(): jnp.einsum('cdts,bdks->bckt', tensor_im, flows, precision=lax.Precision.H...]
    reshape x4 -> x0, local copies, waits for them, and re-layouts: 5.48 us -> none  [the longest x1 4.05 us: make_folder(): flows.reshape(planes, block_count, block_width).transpose(1, 0, 2)]
    dynamic_slice x16 -> x0, local copies, waits for them, and re-layouts: 4.56 us -> none  [make_folder(): accumulated, unused = lax.scan(advance, running, (flow_blocks, spot_blocks))]
  transfers between devices with their start and end apart: 1 -> 0, of which waited for: 0 -> 0; matrix products, arithmetic and copies ran while one was open for 1% -> 0% of each run, Pallas kernels for 0% -> 0%
where the time goes in v1:
time: 57.1 us; the launch traced here: 56.9 us
  Pallas kernels  52.7 us (92%)
  local copies, waits for them, and re-layouts  3.52 us (6%)
  between operations  0.66 us (1%)
    pallas_call x1, Pallas kernels, local(): pl.pallas_call(functools.partial(body, R, C), out_shape=(shape, shape), i...  52.7 us
    unnamed x13, local copies, waits for them, and re-layouts  2.18 us
    pallas_call x2, local copies, waits for them, and re-layouts, local(): pl.pallas_call(functools.partial(body, R, C), out_shape=(shape, shape), i...  1.34 us

profile of v1, /device:TPU:1, one launch (start us, length us, event | category | flops | bytes accessed | tf_op | source)
XLA Modules:
  0.0 56.9 jit_solution(15540206692732376044)
XLA Ops:
  0.6 0.0 copy-start.3
  0.6 0.8 %copy.8.cur_hbm = f32[96,16]{1,0:T(8,128)S(1)} copy(f32[96,16]{0,1:T(8,128)} %param.6) | data formatting | bytes 12288 | tf_op args[0]
  1.4 0.0 copy-done.3
  1.4 0.0 copy-start.4
  1.5 0.1 copy.9.res_hbm
  1.5 0.6 %copy-done.4 = f32[96,16]{0,1:T(8,128)S(1)} copy-done((f32[96,16]{0,1:T(8,128)S(1)}, f32[96,16]{0,1:T(8,128)}, u32[]{:S(2)}) %copy-start.4) | copy-done | bytes 6168
  2.1 0.0 copy-start
  2.1 0.0 copy-start.1
  2.1 0.0 copy-start.2
  2.1 0.1 copy.10.sha_hbm
  2.2 0.6 %copy-done = s32[3,16]{1,0:T(4,128)S(1)} copy-done((s32[3,16]{1,0:T(4,128)S(1)}, s32[3,16]{1,0:T(4,128)}, u32[]{:S(2)}) %copy-start) | copy-done | bytes 216
  2.8 0.0 copy-done.1
  2.8 0.0 copy-done.2
  2.8 52.7 %shard_map.77 = (f32[96,16]{1,0:T(8,128)S(1)}, f32[96,16]{1,0:T(8,128)S(1)}) custom-call(f32[96,16]{1,0:T(8,128)S(1)} %copy.8.cur_hbm, f32[96,16]{1,0:T(8,128)S(1)} %copy.9.res_hbm, f32[96,16]{1,0:T(8,128)S(1)} %copy.10.sha_hbm, s32[3,16]{1,0:T(4,128)S(1)} %copy-done, s32[1,16]{1,0:T(1,128)S(1)} %bitcast.1, f32[2,4]{1,0:T(2,128)S(1)} %copy-done.1), custom_call_target="tpu_custom_call" | custom-call | tf_op jit(solution)/shard_map/pallas_call | solution.py:265
  55.5 0.7 %copy.11 = f32[96,16]{0,1:T(8,128)} copy(f32[96,16]{1,0:T(8,128)S(1)} %get-tuple-element.2) | data formatting | bytes 12288 | tf_op jit(solution)/shard_map/pallas_call | solution.py:265
  56.2 0.7 %copy.12 = f32[96,16]{0,1:T(8,128)} copy(f32[96,16]{1,0:T(8,128)S(1)} %get-tuple-element.3) | data formatting | bytes 12288 | tf_op jit(solution)/shard_map/pallas_call | solution.py:265
Async XLA Ops:
  0.6 0.8 %copy-start.3 = (f32[96,16]{0,1:T(8,128)S(1)}, f32[96,16]{0,1:T(8,128)}, u32[]{:S(2)}) copy-start(f32[96,16]{0,1:T(8,128)} %param.7) | copy-start | bytes 18436
  1.4 0.7 %copy-start.4 = (f32[96,16]{0,1:T(8,128)S(1)}, f32[96,16]{0,1:T(8,128)}, u32[]{:S(2)}) copy-start(f32[96,16]{0,1:T(8,128)} %param.8) | copy-start | bytes 18436
  2.1 0.7 %copy-start = (s32[3,16]{1,0:T(4,128)S(1)}, s32[3,16]{1,0:T(4,128)}, u32[]{:S(2)}) copy-start(s32[3,16]{1,0:T(4,128)} %site_hbm.1) | copy-start | bytes 580
  2.1 0.7 %copy-start.1 = (f32[2,4]{1,0:T(2,128)S(1)}, f32[2,4]{1,0:T(2,128)}, u32[]{:S(2)}) copy-start(f32[2,4]{1,0:T(2,128)} %pol_hbm.1) | copy-start | bytes 100
  2.1 0.7 %copy-start.2 = (s32[16]{0:T(128)S(1)}, s32[16]{0:T(128)}, u32[]{:S(2)}) copy-start(s32[16]{0:T(128)} %param.10) | copy-start | bytes 196

commit v2 on v1

v2 whole, which is shorter than its diff:
```python
import functools
import math

import jax
import jax.numpy as jnp
import numpy as np
from jax import lax
from jax.experimental import pallas as pl
from jax.experimental.pallas import tpu as pltpu
from jax.sharding import PartitionSpec as P

MESH = pl.DeviceIdType.MESH
K = 0.9
SH = 16
PLANES = 96
PAIRS = ((0, 0), (1, 1), (2, 2), (0, 1), (0, 2), (1, 2))


def _fit(terms, odd):
    nodes = 0.5 * np.cos((np.arange(400) + 0.5) * np.pi / 400)
    powers = np.arange(terms) * 2 + (1 if odd else 0)
    values = np.sin(2 * np.pi * nodes) if odd else np.cos(2 * np.pi * nodes)
    solved = np.linalg.lstsq(nodes[:, None] ** powers[None, :], values, rcond=None)[0]
    return [float(x) for x in solved]


SIN = _fit(6, True)
COS = _fit(7, False)


def _horner(coefs, x):
    out = jnp.float32(coefs[-1])
    for coef in coefs[-2::-1]:
        out = out * x + jnp.float32(coef)
    return out


def green(tx, ty, tz, sx, sy, sz):
    dx, dy, dz = tx - sx, ty - sy, tz - sz
    xx, yy, zz = dx * dx, dy * dy, dz * dz
    dist_sq = xx + yy + zz
    safe = jnp.maximum(dist_sq, 1.0)
    inv = lax.rsqrt(safe)
    dist = safe * inv
    reach = inv * jnp.minimum(dist_sq, 1.0)
    turns = dist * jnp.float32(K / (2 * math.pi))
    frac = turns - jnp.round(turns)
    frac_sq = frac * frac
    e_re = _horner(COS, frac_sq) * reach
    e_im = _horner(SIN, frac_sq) * frac * reach
    inv_sq = inv * inv
    iso_re = jnp.float32(K * K) - inv_sq
    iso_im = jnp.float32(K) * inv
    a_re = e_re * iso_re - e_im * iso_im
    a_im = e_im * iso_re + e_re * iso_im
    b_re = (jnp.float32(2 * K * K) * e_re - 3.0 * a_re) * inv_sq
    b_im = (jnp.float32(2 * K * K) * e_im - 3.0 * a_im) * inv_sq
    outer = (xx, yy, zz, dx * dy, dx * dz, dy * dz)
    parts = []
    for place, product in enumerate(outer):
        re, im = product * b_re, product * b_im
        if place < 3:
            re, im = re + a_re, im + a_im
        parts.extend((re, im))
    return parts


def rows(array, b, component):
    start = b * 48 + component * 16
    return array[start : start + 16]


def lanes(height):
    return lax.broadcasted_iota(jnp.int32, (height, 128), 1)


def sublanes(height):
    return lax.broadcasted_iota(jnp.int32, (height, 128), 0)


def swapped(block):
    lane = lanes(block.shape[0])
    turned = jnp.where(lane < 48, -pltpu.roll(block, 80, 1), pltpu.roll(block, 48, 1))
    return jnp.where(lane < PLANES, turned, 0.0)


def fold(block):
    for shift in (64, 32, 16):
        block = block + pltpu.roll(block, shift, 1)
    return block


def body(
    Z, C,
    cur_hbm, res_hbm, sha_hbm, site_hbm, cls_hbm, pol_hbm,
    img_out, half_out,
    cur, res, sha, site, cls, pol,
    wide, src_all, spot_all, tgt_all, tgt_t, ghi, glo, rs_send, rs_recv, den_all, fin_all,
    in_sems, send_sems, recv_sems,
):
    r, c = lax.axis_index("row"), lax.axis_index("col")
    z, core = r // 2, r % 2
    D = 2 * C
    q = core * C + c
    T, S = D * SH, Z * SH

    def plane_peer(i):
        other = lax.rem(q + i, D)
        return other, {"row": z * 2 + other // C, "col": other % C}

    def far_peer(i):
        step = jnp.where(i % 2 == 1, Z // 2 + i // 2, Z // 2 - i // 2)
        return {"row": lax.rem(z + step, Z) * 2 + core}

    pairs = ((cur_hbm, cur), (res_hbm, res), (sha_hbm, sha), (site_hbm, site), (cls_hbm, cls), (pol_hbm, pol))
    loads = [pltpu.make_async_copy(a, b, in_sems.at[i]) for i, (a, b) in enumerate(pairs)]
    for load in loads:
        load.start()

    barrier = pltpu.get_barrier_semaphore()

    def greet_far(i, carry):
        pl.semaphore_signal(barrier, inc=1, device_id=far_peer(i), device_id_type=MESH)
        return carry

    def greet_plane(i, carry):
        pl.semaphore_signal(barrier, inc=1, device_id=plane_peer(i)[1], device_id_type=MESH)
        return carry

    lax.fori_loop(1, Z, greet_far, 0)
    lax.fori_loop(1, D, greet_plane, 0)

    wide[...] = jnp.zeros_like(wide)
    for load in loads:
        load.wait()

    for i, ref in enumerate((cur, res, sha)):
        wide[i, :, 0:PLANES] = ref[...]
    lane, sublane = lanes(SH), sublanes(SH)
    group, diagonal = lane // 16, lane % 16 == sublane
    small_lane = lax.broadcasted_iota(jnp.int32, (SH, SH), 1)
    small_sublane = lax.broadcasted_iota(jnp.int32, (SH, SH), 0)

    def column(row):
        return jnp.sum(jnp.where(small_lane == small_sublane, row, 0.0), axis=1, keepdims=True)

    flow, resid, shade = wide[0], wide[1], wide[2]
    spots = site[...].astype(jnp.float32)
    axes = [column(spots[i : i + 1]) for i in range(3)]
    block = shade
    spot_row = jnp.zeros((SH, 128), jnp.float32)
    for i in range(3):
        block = jnp.where(lane == PLANES + i, axes[i], block)
        spot_row = jnp.where((group == i) & diagonal, axes[i], spot_row)
    tgt_all[q] = block
    spot_all[z] = jnp.sum(spot_row, axis=0, keepdims=True)
    src_all[z] = flow

    def copy(which, src, dst, device_id):
        return pltpu.make_async_remote_copy(
            src_ref=src, dst_ref=dst, send_sem=send_sems.at[which], recv_sem=recv_sems.at[which],
            device_id=device_id, device_id_type=MESH,
        )

    def send_spot(i, carry):
        copy(0, spot_all.at[z], spot_all.at[z], far_peer(i)).start()
        return carry

    def send_tgt(i, carry):
        copy(1, tgt_all.at[q], tgt_all.at[q], plane_peer(i)[1]).start()
        return carry

    def send_src(i, carry):
        copy(2, src_all.at[z], src_all.at[z], far_peer(i)).start()
        return carry

    def drain(which, buffer, count):
        whole = buffer.at[pl.ds(0, count)]
        copy(which, whole, whole, far_peer(1)).wait()

    pl.semaphore_wait(barrier, Z + D - 2)
    lax.fori_loop(1, Z, send_spot, 0)
    lax.fori_loop(1, D, send_tgt, 0)
    lax.fori_loop(1, Z, send_src, 0)

    class_col = column(cls[...].astype(jnp.float32))
    pol_re = jnp.zeros((SH, 1), jnp.float32)
    pol_im = jnp.zeros((SH, 1), jnp.float32)
    for kind in range(pol.shape[1]):
        pol_re = jnp.where(class_col == kind, pol[0:1, kind : kind + 1], pol_re)
        pol_im = jnp.where(class_col == kind, pol[1:2, kind : kind + 1], pol_im)
    own = pol_re * flow + pol_im * swapped(flow)
    turned_shade = swapped(shade)
    sums = [
        jnp.sum(product, axis=0, keepdims=True)
        for product in (shade * own, turned_shade * own, shade * resid, turned_shade * resid)
    ]
    eight = lax.broadcasted_iota(jnp.int32, (8, 128), 0)
    stacked = jnp.zeros((8, 128), jnp.float32)
    for i, row in enumerate(sums):
        stacked = jnp.where(eight == i, row, stacked)
    stacked = fold(stacked)
    eight_group = lanes(8) // 16
    own_row = jnp.sum(jnp.where(eight_group == eight, stacked, 0.0), axis=0, keepdims=True)

    drain(1, tgt_all, D - 1)
    tgt_t[...] = tgt_all[...].reshape(T, 128).T
    drain(0, spot_all, Z - 1)

    def fill(j, carry):
        row = spot_all[j]
        sx, sy, sz = (
            jnp.sum(jnp.where((group == i) & diagonal, row, 0.0), axis=1, keepdims=True) for i in range(3)
        )
        place = pl.ds(pl.multiple_of(j * SH, SH), SH)
        for part in range(2):
            cols = slice(part * (T // 2), (part + 1) * (T // 2))
            tx, ty, tz = (tgt_t[PLANES + i : PLANES + i + 1, cols] for i in range(3))
            for which, value in enumerate(green(tx, ty, tz, sx, sy, sz)):
                high = value.astype(jnp.bfloat16)
                ghi[which, place, cols] = high
                glo[which, place, cols] = (value - high.astype(jnp.float32)).astype(jnp.bfloat16)
        return carry

    lax.fori_loop(0, Z, fill, 0)
    drain(2, src_all, Z - 1)

    flows = src_all[...].reshape(S, 128).T
    f_hi = flows.astype(jnp.bfloat16)
    f_lo = (flows - f_hi.astype(jnp.float32)).astype(jnp.bfloat16)

    def two(array, comp):
        return [rows(array, 0, comp), rows(array, 1, comp)]

    sums = [[0.0, 0.0, 0.0], [0.0, 0.0, 0.0]]
    for which, (a, b) in enumerate(PAIRS):
        high = two(f_hi, a) if a == b else two(f_hi, b) + two(f_hi, a)
        low = two(f_lo, a) if a == b else two(f_lo, b) + two(f_lo, a)
        height = 16 * len(high)
        both = jnp.concatenate(high + low, axis=0)
        high = both[:height]
        for part in range(2):
            one = jnp.dot(both, ghi[2 * which + part], preferred_element_type=jnp.float32)
            other = jnp.dot(high, glo[2 * which + part], preferred_element_type=jnp.float32)
            got = one[:height] + one[height:] + other
            sums[part][a] = sums[part][a] + got[:32]
            if a != b:
                sums[part][b] = sums[part][b] + got[32:]

    field_re = [sums[0][i][:16] - sums[1][i][16:] for i in range(3)]
    field_im = [sums[0][i][16:] + sums[1][i][:16] for i in range(3)]
    den_re = den_im = 0.0
    for i in range(3):
        sr, si = rows(tgt_t, 0, i), rows(tgt_t, 1, i)
        den_re = den_re + sr * field_re[i] + si * field_im[i]
        den_im = den_im + sr * field_im[i] - si * field_re[i]
    den_re = jnp.sum(den_re, axis=1, keepdims=True)
    den_im = jnp.sum(den_im, axis=1, keepdims=True)
    spread = jnp.where(group == 0, den_re, jnp.where(group == 1, den_im, 0.0))
    den_all[q] = own_row - jnp.sum(jnp.where(diagonal, spread, 0.0), axis=0, keepdims=True)

    def send_den(i, carry):
        copy(3, den_all.at[q], den_all.at[q], plane_peer(i)[1]).start()
        return carry

    def send_field(i, carry):
        other, device_id = plane_peer(i)
        copy(4, rs_send.at[other], rs_recv.at[q], device_id).start()
        return carry

    def send_fin(i, carry):
        copy(5, fin_all.at[z], fin_all.at[z], far_peer(i)).start()
        return carry

    lax.fori_loop(1, D, send_den, 0)
    partial = jnp.concatenate(field_re + field_im + [jnp.zeros((32, T), jnp.float32)], axis=0)
    rs_send[...] = partial.T.reshape(D, SH, 128)
    lax.fori_loop(1, D, send_field, 0)
    rs_recv[q] = rs_send[q]
    drain(3, den_all, D - 1)
    fin_all[z] = jnp.sum(den_all[...], axis=0)
    lax.fori_loop(1, Z, send_fin, 0)
    drain(4, rs_recv, D - 1)
    image = own - jnp.sum(rs_recv[...], axis=0)
    turned = swapped(image)
    img_out[...] = image[:, 0:PLANES]

    drain(5, fin_all, Z - 1)
    ends = jnp.sum(fin_all[...], axis=0)
    ends = fold(jnp.where(eight_group == eight, ends, 0.0))
    den_re, den_im, rho_re, rho_im = (ends[i : i + 1] for i in range(4))
    magnitude = jnp.maximum(den_re * den_re + den_im * den_im, 1.0)
    alpha_re = (rho_re * den_re + rho_im * den_im) / magnitude
    alpha_im = (rho_im * den_re - rho_re * den_im) / magnitude
    half_out[...] = (resid - (alpha_re * image + alpha_im * turned))[:, 0:PLANES]


def local(R, C, currents, residual, shadow, lattice_sites, classes, inverse_polarizability):
    f32 = jnp.float32
    Z, D = R // 2, 2 * C
    T, S = D * SH, Z * SH
    shape = jax.ShapeDtypeStruct((SH, PLANES), f32)
    image, half = pl.pallas_call(
        functools.partial(body, Z, C),
        out_shape=(shape, shape),
        in_specs=[pl.BlockSpec(memory_space=pltpu.HBM)] * 6,
        out_specs=(pl.BlockSpec(memory_space=pltpu.VMEM), pl.BlockSpec(memory_space=pltpu.VMEM)),
        scratch_shapes=[
            pltpu.VMEM((SH, PLANES), f32),
            pltpu.VMEM((SH, PLANES), f32),
            pltpu.VMEM((SH, PLANES), f32),
            pltpu.VMEM((3, SH), jnp.int32),
            pltpu.VMEM((1, SH), jnp.int32),
            pltpu.VMEM(inverse_polarizability.shape, f32),
            pltpu.VMEM((3, SH, 128), f32),
            pltpu.VMEM((Z, SH, 128), f32),
            pltpu.VMEM((Z, 1, 128), f32),
            pltpu.VMEM((D, SH, 128), f32),
            pltpu.VMEM((128, T), f32),
            pltpu.VMEM((12, S, T), jnp.bfloat16),
            pltpu.VMEM((12, S, T), jnp.bfloat16),
            pltpu.VMEM((D, SH, 128), f32),
            pltpu.VMEM((D, SH, 128), f32),
            pltpu.VMEM((D, 1, 128), f32),
            pltpu.VMEM((Z, 1, 128), f32),
            pltpu.SemaphoreType.DMA((6,)),
            pltpu.SemaphoreType.DMA((6,)),
            pltpu.SemaphoreType.DMA((6,)),
        ],
        compiler_params=pltpu.CompilerParams(
            collective_id=0, has_side_effects=True, vmem_limit_bytes=62 * 1024 * 1024
        ),
    )(currents.T, residual.T, shadow.T, lattice_sites, classes.reshape(1, SH), inverse_polarizability)
    return image.T, half.T


def solution(mesh):
    both = ("row", "col")
    in_specs = (P(None, both), P(None, both), P(None, both), P(None, both), P(both), P())
    out_specs = (P(None, both), P(None, both))
    step = functools.partial(local, mesh.shape["row"], mesh.shape["col"])
    return jax.shard_map(step, mesh=mesh, in_specs=in_specs, out_specs=out_specs, check_vma=False)
```

time: 57.1 us -> 44.3 us (0.78)
  Pallas kernels: 52.7 us -> 41.6 us
  local copies, waits for them, and re-layouts: 3.52 us -> 1.9 us
    pallas_call x1, Pallas kernels: 52.7 us -> 41.6 us  [local(): pl.pallas_call(functools.partial(body, Z, C), out_shape=(shape, shape), i...]
    pallas_call x2 -> x0, local copies, waits for them, and re-layouts: 1.34 us -> none  [local(): pl.pallas_call(functools.partial(body, R, C), out_shape=(shape, shape), i...]
    unnamed x13 -> x4, local copies, waits for them, and re-layouts: 2.18 us -> 1.9 us
where the time goes in v2:
time: 44.3 us; the launch traced here: 44.2 us
  Pallas kernels  41.6 us (94%)
  local copies, waits for them, and re-layouts  1.9 us (4%)
  between operations  0.65 us (1%)
    pallas_call x1, Pallas kernels, local(): pl.pallas_call(functools.partial(body, Z, C), out_shape=(shape, shape), i...  41.6 us
    unnamed x4, local copies, waits for them, and re-layouts  1.9 us

profile of v2, /device:TPU:1, one launch (start us, length us, event | category | flops | bytes accessed | tf_op | source)
XLA Modules:
  0.0 44.2 jit_solution(6374855215118469669)
XLA Ops:
  0.6 41.6 %shard_map.77 = (f32[16,96]{1,0:T(8,128)}, f32[16,96]{1,0:T(8,128)}) custom-call(f32[16,96]{1,0:T(8,128)} %bitcast.6, f32[16,96]{1,0:T(8,128)} %bitcast.7, f32[16,96]{1,0:T(8,128)} %bitcast.8, s32[3,16]{1,0:T(4,128)} %site_hbm.1, s32[1,16]{1,0:T(1,128)} %bitcast.11, f32[2,4]{1,0:T(2,128)} %pol_hbm.1), custom_call_target="tpu_custom_call" | custom-call | tf_op jit(solution)/shard_map/pallas_call | solution.py:303
  42.3 0.0 copy-start
  42.3 1.3 %copy.10 = f32[96,16]{0,1:T(8,128)} copy(f32[96,16]{0,1:T(8,128)} %bitcast.10) | data formatting | bytes 12288
  43.6 0.0 copy-done
  43.6 0.6 %copy.11 = f32[96,16]{0,1:T(8,128)} copy(f32[96,16]{0,1:T(8,128)S(1)} %bitcast.9) | data formatting | bytes 12288
Async XLA Ops:
  42.3 1.3 %copy-start = (f32[16,96]{1,0:T(8,128)S(1)}, f32[16,96]{1,0:T(8,128)}, u32[]{:S(2)}) copy-start(f32[16,96]{1,0:T(8,128)} %get-tuple-element.5) | copy-start | bytes 18436

commit v3 on v2

--- a/solution.py
+++ b/solution.py
@@ -95,7 +95,7 @@
     cur_hbm, res_hbm, sha_hbm, site_hbm, cls_hbm, pol_hbm,
     img_out, half_out,
     cur, res, sha, site, cls, pol,
-    wide, src_all, spot_all, tgt_all, tgt_t, ghi, glo, rs_send, rs_recv, den_all, fin_all,
+    wide, src_all, spot_all, here_all, axes_t, axes_s, tgt_all, tgt_t, fields, ghi, glo, rs_send, rs_recv, den_all, fin_all,
     in_sems, send_sems, recv_sems,
 ):
     r, c = lax.axis_index("row"), lax.axis_index("col")
@@ -104,13 +104,19 @@
     q = core * C + c
     T, S = D * SH, Z * SH
 
+    def wrap(i, size):
+        return jnp.where(i >= size, i - size, i)
+
     def plane_peer(i):
-        other = lax.rem(q + i, D)
-        return other, {"row": z * 2 + other // C, "col": other % C}
+        other = wrap(q + i, D)
+        upper = other >= C
+        return other, {"row": z * 2 + jnp.where(upper, 1, 0), "col": jnp.where(upper, other - C, other)}
+
+    HALF, OWN = Z // 2, Z // 4
 
     def far_peer(i):
-        step = jnp.where(i % 2 == 1, Z // 2 + i // 2, Z // 2 - i // 2)
-        return {"row": lax.rem(z + step, Z) * 2 + core}
+        step = jnp.where(i % 2 == 0, HALF + i // 2, HALF - i // 2)
+        return wrap(OWN - step + Z, Z), {"row": wrap(z + step, Z) * 2 + core}
 
     pairs = ((cur_hbm, cur), (res_hbm, res), (sha_hbm, sha), (site_hbm, site), (cls_hbm, cls), (pol_hbm, pol))
     loads = [pltpu.make_async_copy(a, b, in_sems.at[i]) for i, (a, b) in enumerate(pairs)]
@@ -120,7 +126,7 @@
     barrier = pltpu.get_barrier_semaphore()
 
     def greet_far(i, carry):
-        pl.semaphore_signal(barrier, inc=1, device_id=far_peer(i), device_id_type=MESH)
+        pl.semaphore_signal(barrier, inc=1, device_id=far_peer(i)[1], device_id_type=MESH)
         return carry
 
     def greet_plane(i, carry):
@@ -153,8 +159,10 @@
         block = jnp.where(lane == PLANES + i, axes[i], block)
         spot_row = jnp.where((group == i) & diagonal, axes[i], spot_row)
     tgt_all[q] = block
-    spot_all[z] = jnp.sum(spot_row, axis=0, keepdims=True)
-    src_all[z] = flow
+    spot_row = jnp.sum(spot_row, axis=0, keepdims=True)
+    spot_all[OWN] = spot_row
+    here_all[q] = spot_row
+    src_all[OWN] = flow
 
     def copy(which, src, dst, device_id):
         return pltpu.make_async_remote_copy(
@@ -162,26 +170,27 @@
             device_id=device_id, device_id_type=MESH,
         )
 
-    def send_spot(i, carry):
-        copy(0, spot_all.at[z], spot_all.at[z], far_peer(i)).start()
+    def send_here(i, carry):
+        copy(0, here_all.at[q], here_all.at[q], plane_peer(i)[1]).start()
+        return carry
+
+    def send_spot(which, i, carry):
+        slot, device_id = far_peer(i)
+        copy(which, spot_all.at[OWN], spot_all.at[slot], device_id).start()
+        return carry
+
+    def send_src(which, i, carry):
+        slot, device_id = far_peer(i)
+        copy(which, src_all.at[OWN], src_all.at[slot], device_id).start()
         return carry
 
     def send_tgt(i, carry):
-        copy(1, tgt_all.at[q], tgt_all.at[q], plane_peer(i)[1]).start()
-        return carry
-
-    def send_src(i, carry):
-        copy(2, src_all.at[z], src_all.at[z], far_peer(i)).start()
+        copy(5, tgt_all.at[q], tgt_all.at[q], plane_peer(i)[1]).start()
         return carry
 
     def drain(which, buffer, count):
         whole = buffer.at[pl.ds(0, count)]
-        copy(which, whole, whole, far_peer(1)).wait()
-
-    pl.semaphore_wait(barrier, Z + D - 2)
-    lax.fori_loop(1, Z, send_spot, 0)
-    lax.fori_loop(1, D, send_tgt, 0)
-    lax.fori_loop(1, Z, send_src, 0)
+        copy(which, whole, whole, far_peer(1)[1]).wait()
 
     class_col = column(cls[...].astype(jnp.float32))
     pol_re = jnp.zeros((SH, 1), jnp.float32)
@@ -203,89 +212,121 @@
     eight_group = lanes(8) // 16
     own_row = jnp.sum(jnp.where(eight_group == eight, stacked, 0.0), axis=0, keepdims=True)
 
-    drain(1, tgt_all, D - 1)
-    tgt_t[...] = tgt_all[...].reshape(T, 128).T
-    drain(0, spot_all, Z - 1)
+    pl.semaphore_wait(barrier, Z + D - 2)
+    lax.fori_loop(1, D, send_here, 0)
+    lax.fori_loop(HALF + 1, Z, functools.partial(send_spot, 1), 0)
+    lax.fori_loop(1, HALF + 1, functools.partial(send_spot, 2), 0)
+    lax.fori_loop(1, HALF + 1, functools.partial(send_src, 3), 0)
+    lax.fori_loop(HALF + 1, Z, functools.partial(send_src, 4), 0)
+    lax.fori_loop(1, D, send_tgt, 0)
+
+    drain(0, here_all, D - 1)
+    for part in range(T // 128):
+        eight_rows = here_all[part * 8 : part * 8 + 8].reshape(8, 128)
+        for i in range(3):
+            tiled = fold(jnp.where(eight_group == i, eight_rows, 0.0))
+            picked = jnp.sum(jnp.where(eight_group == eight, tiled, 0.0), axis=0, keepdims=True)
+            axes_t[i : i + 1, part * 128 : part * 128 + 128] = picked
+
+    def spread_spots(j, carry):
+        row = spot_all[j]
+        for i in range(3):
+            col = jnp.sum(jnp.where((group == i) & diagonal, row, 0.0), axis=1, keepdims=True)
+            axes_s[i, pl.ds(pl.multiple_of(j * SH, SH), SH), :] = jnp.broadcast_to(col, (SH, 128))
+        return carry
 
     def fill(j, carry):
-        row = spot_all[j]
-        sx, sy, sz = (
-            jnp.sum(jnp.where((group == i) & diagonal, row, 0.0), axis=1, keepdims=True) for i in range(3)
-        )
         place = pl.ds(pl.multiple_of(j * SH, SH), SH)
+        wide_t = T // 2
+        sx, sy, sz = (jnp.tile(axes_s[i, place, :], (1, wide_t // 128)) for i in range(3))
         for part in range(2):
-            cols = slice(part * (T // 2), (part + 1) * (T // 2))
-            tx, ty, tz = (tgt_t[PLANES + i : PLANES + i + 1, cols] for i in range(3))
+            cols = slice(part * wide_t, (part + 1) * wide_t)
+            tx, ty, tz = (axes_t[i : i + 1, cols] for i in range(3))
             for which, value in enumerate(green(tx, ty, tz, sx, sy, sz)):
                 high = value.astype(jnp.bfloat16)
                 ghi[which, place, cols] = high
                 glo[which, place, cols] = (value - high.astype(jnp.float32)).astype(jnp.bfloat16)
         return carry
 
-    lax.fori_loop(0, Z, fill, 0)
-    drain(2, src_all, Z - 1)
-
-    flows = src_all[...].reshape(S, 128).T
-    f_hi = flows.astype(jnp.bfloat16)
-    f_lo = (flows - f_hi.astype(jnp.float32)).astype(jnp.bfloat16)
-
     def two(array, comp):
         return [rows(array, 0, comp), rows(array, 1, comp)]
 
-    sums = [[0.0, 0.0, 0.0], [0.0, 0.0, 0.0]]
-    for which, (a, b) in enumerate(PAIRS):
-        high = two(f_hi, a) if a == b else two(f_hi, b) + two(f_hi, a)
-        low = two(f_lo, a) if a == b else two(f_lo, b) + two(f_lo, a)
-        height = 16 * len(high)
-        both = jnp.concatenate(high + low, axis=0)
-        high = both[:height]
-        for part in range(2):
-            one = jnp.dot(both, ghi[2 * which + part], preferred_element_type=jnp.float32)
-            other = jnp.dot(high, glo[2 * which + part], preferred_element_type=jnp.float32)
-            got = one[:height] + one[height:] + other
-            sums[part][a] = sums[part][a] + got[:32]
-            if a != b:
-                sums[part][b] = sums[part][b] + got[32:]
-
-    field_re = [sums[0][i][:16] - sums[1][i][16:] for i in range(3)]
-    field_im = [sums[0][i][16:] + sums[1][i][:16] for i in range(3)]
+    def products(part):
+        span = slice(part * (S // 2), (part + 1) * (S // 2))
+        flows = src_all[part * HALF : (part + 1) * HALF].reshape(S // 2, 128).T
+        f_hi = flows.astype(jnp.bfloat16)
+        f_lo = (flows - f_hi.astype(jnp.float32)).astype(jnp.bfloat16)
+        sums = [[0.0, 0.0, 0.0], [0.0, 0.0, 0.0]]
+        for which, (a, b) in enumerate(PAIRS):
+            high = two(f_hi, a) if a == b else two(f_hi, b) + two(f_hi, a)
+            low = two(f_lo, a) if a == b else two(f_lo, b) + two(f_lo, a)
+            height = 16 * len(high)
+            both = jnp.concatenate(high + low, axis=0)
+            high = both[:height]
+            for ri in range(2):
+                one = jnp.dot(both, ghi[2 * which + ri, span, :], preferred_element_type=jnp.float32)
+                other = jnp.dot(high, glo[2 * which + ri, span, :], preferred_element_type=jnp.float32)
+                got = one[:height] + one[height:] + other
+                sums[ri][a] = sums[ri][a] + got[:32]
+                if a != b:
+                    sums[ri][b] = sums[ri][b] + got[32:]
+        field_re = [sums[0][i][:16] - sums[1][i][16:] for i in range(3)]
+        field_im = [sums[0][i][16:] + sums[1][i][:16] for i in range(3)]
+        return field_re + field_im
+
+    drain(1, spot_all, Z - 1 - HALF)
+    lax.fori_loop(0, HALF, spread_spots, 0, unroll=True)
+    lax.fori_loop(0, HALF, fill, 0)
+    drain(2, spot_all, HALF)
+    lax.fori_loop(HALF, Z, spread_spots, 0, unroll=True)
+    lax.fori_loop(HALF, Z, fill, 0)
+    drain(4, src_all, Z - 1 - HALF)
+    fields[0:PLANES, :] = jnp.concatenate(products(0), axis=0)
+    fields[PLANES:128, :] = jnp.zeros((128 - PLANES, T), jnp.float32)
+    drain(5, tgt_all, D - 1)
+    tgt_t[...] = tgt_all[...].reshape(T, 128).T
+    drain(3, src_all, HALF)
+    parts = products(1)
     den_re = den_im = 0.0
     for i in range(3):
         sr, si = rows(tgt_t, 0, i), rows(tgt_t, 1, i)
-        den_re = den_re + sr * field_re[i] + si * field_im[i]
-        den_im = den_im + sr * field_im[i] - si * field_re[i]
+        re, im = rows(fields, 0, i) + parts[i], rows(fields, 1, i) + parts[3 + i]
+        den_re = den_re + sr * re + si * im
+        den_im = den_im + sr * im - si * re
+        fields[i * 16 : i * 16 + 16, :] = re
+        fields[48 + i * 16 : 64 + i * 16, :] = im
     den_re = jnp.sum(den_re, axis=1, keepdims=True)
     den_im = jnp.sum(den_im, axis=1, keepdims=True)
     spread = jnp.where(group == 0, den_re, jnp.where(group == 1, den_im, 0.0))
     den_all[q] = own_row - jnp.sum(jnp.where(diagonal, spread, 0.0), axis=0, keepdims=True)
 
     def send_den(i, carry):
-        copy(3, den_all.at[q], den_all.at[q], plane_peer(i)[1]).start()
+        copy(6, den_all.at[q], den_all.at[q], plane_peer(i)[1]).start()
         return carry
 
     def send_field(i, carry):
         other, device_id = plane_peer(i)
-        copy(4, rs_send.at[other], rs_recv.at[q], device_id).start()
+        copy(7, rs_send.at[other], rs_recv.at[q], device_id).start()
         return carry
 
     def send_fin(i, carry):
-        copy(5, fin_all.at[z], fin_all.at[z], far_peer(i)).start()
+        slot, device_id = far_peer(i)
+        copy(8, fin_all.at[OWN], fin_all.at[slot], device_id).start()
         return carry
 
     lax.fori_loop(1, D, send_den, 0)
-    partial = jnp.concatenate(field_re + field_im + [jnp.zeros((32, T), jnp.float32)], axis=0)
-    rs_send[...] = partial.T.reshape(D, SH, 128)
+    rs_send[...] = fields[...].T.reshape(D, SH, 128)
     lax.fori_loop(1, D, send_field, 0)
     rs_recv[q] = rs_send[q]
-    drain(3, den_all, D - 1)
-    fin_all[z] = jnp.sum(den_all[...], axis=0)
+    drain(6, den_all, D - 1)
+    fin_all[OWN] = jnp.sum(den_all[...], axis=0)
     lax.fori_loop(1, Z, send_fin, 0)
-    drain(4, rs_recv, D - 1)
+    drain(7, rs_recv, D - 1)
     image = own - jnp.sum(rs_recv[...], axis=0)
     turned = swapped(image)
     img_out[...] = image[:, 0:PLANES]
 
-    drain(5, fin_all, Z - 1)
+    drain(8, fin_all, Z - 1)
     ends = jnp.sum(fin_all[...], axis=0)
     ends = fold(jnp.where(eight_group == eight, ends, 0.0))
     den_re, den_im, rho_re, rho_im = (ends[i : i + 1] for i in range(4))
@@ -295,14 +336,22 @@
     half_out[...] = (resid - (alpha_re * image + alpha_im * turned))[:, 0:PLANES]
 
 
+def deliver(image, half, image_out, half_out, sems):
+    copies = [pltpu.make_async_copy(image, image_out, sems.at[0]), pltpu.make_async_copy(half, half_out, sems.at[1])]
+    for one in copies:
+        one.start()
+    for one in copies:
+        one.wait()
+
+
 def local(R, C, currents, residual, shadow, lattice_sites, classes, inverse_polarizability):
     f32 = jnp.float32
     Z, D = R // 2, 2 * C
     T, S = D * SH, Z * SH
     shape = jax.ShapeDtypeStruct((SH, PLANES), f32)
-    image, half = pl.pallas_call(
+    blocks = pl.pallas_call(
         functools.partial(body, Z, C),
-        out_shape=(shape, shape),
+        out_shape=(pltpu.VMEM((SH, PLANES), f32), pltpu.VMEM((SH, PLANES), f32)),
         in_specs=[pl.BlockSpec(memory_space=pltpu.HBM)] * 6,
         out_specs=(pl.BlockSpec(memory_space=pltpu.VMEM), pl.BlockSpec(memory_space=pltpu.VMEM)),
         scratch_shapes=[
@@ -315,7 +364,11 @@
             pltpu.VMEM((3, SH, 128), f32),
             pltpu.VMEM((Z, SH, 128), f32),
             pltpu.VMEM((Z, 1, 128), f32),
+            pltpu.VMEM((D, 1, 128), f32),
+            pltpu.VMEM((8, T), f32),
+            pltpu.VMEM((3, S, 128), f32),
             pltpu.VMEM((D, SH, 128), f32),
+            pltpu.VMEM((128, T), f32),
             pltpu.VMEM((128, T), f32),
             pltpu.VMEM((12, S, T), jnp.bfloat16),
             pltpu.VMEM((12, S, T), jnp.bfloat16),
@@ -324,13 +377,20 @@
             pltpu.VMEM((D, 1, 128), f32),
             pltpu.VMEM((Z, 1, 128), f32),
             pltpu.SemaphoreType.DMA((6,)),
-            pltpu.SemaphoreType.DMA((6,)),
-            pltpu.SemaphoreType.DMA((6,)),
+            pltpu.SemaphoreType.DMA((9,)),
+            pltpu.SemaphoreType.DMA((9,)),
         ],
         compiler_params=pltpu.CompilerParams(
             collective_id=0, has_side_effects=True, vmem_limit_bytes=62 * 1024 * 1024
         ),
     )(currents.T, residual.T, shadow.T, lattice_sites, classes.reshape(1, SH), inverse_polarizability)
+    image, half = pl.pallas_call(
+        deliver,
+        out_shape=(shape, shape),
+        in_specs=[pl.BlockSpec(memory_space=pltpu.VMEM)] * 2,
+        out_specs=(pl.BlockSpec(memory_space=pltpu.HBM), pl.BlockSpec(memory_space=pltpu.HBM)),
+        scratch_shapes=[pltpu.SemaphoreType.DMA((2,))],
+    )(*(pltpu.with_memory_space_constraint(block, pltpu.VMEM) for block in blocks))
     return image.T, half.T
 
 

time: 44.3 us -> 41.4 us (0.935)
  local copies, waits for them, and re-layouts: 1.9 us -> 0 us
  Pallas kernels: 41.6 us -> 40.7 us
    unnamed x4 -> x0, local copies, waits for them, and re-layouts: 1.9 us -> none
    pallas_call x1 -> x2, Pallas kernels: 41.6 us -> 40.7 us  [the longest x1 40 us: local(): pl.pallas_call(functools.partial(body, Z, C), out_shape=(pltpu.VMEM((SH,...]
where the time goes in v3:
time: 41.4 us; the launch traced here: 41.3 us
  Pallas kernels  40.7 us (98%)
  between operations  0.64 us (2%)
    pallas_call x1, Pallas kernels, local(): pl.pallas_call(functools.partial(body, Z, C), out_shape=(pltpu.VMEM((SH,...  40 us

profile of v3, /device:TPU:1, one launch (start us, length us, event | category | flops | bytes accessed | tf_op | source)
XLA Modules:
  0.0 41.3 jit_solution(14572093362867575882)
XLA Ops:
  0.6 40.0 %shard_map.77 = (f32[16,96]{1,0:T(8,128)S(1)}, f32[16,96]{1,0:T(8,128)S(1)}) custom-call(f32[16,96]{1,0:T(8,128)} %bitcast.6, f32[16,96]{1,0:T(8,128)} %bitcast.7, f32[16,96]{1,0:T(8,128)} %bitcast.8, s32[3,16]{1,0:T(4,128)} %site_hbm.1, s32[1,16]{1,0:T(1,128)} %bitcast.9, f32[2,4]{1,0:T(2,128)} %pol_hbm.1), custom_call_target="tpu_custom_call" | custom-call | tf_op jit(solution)/shard_map/pallas_call | solution.py:352
  40.7 0.6 %shard_map.78 = (f32[16,96]{1,0:T(8,128)}, f32[16,96]{1,0:T(8,128)}) custom-call(f32[16,96]{1,0:T(8,128)S(1)} %get-tuple-element.6.image, f32[16,96]{1,0:T(8,128)S(1)} %get-tuple-element.7.half), custom_call_target="tpu_custom_call" | custom-call | tf_op jit(solution)/shard_map/pallas_call | solution.py:387

commit v4 on v3

--- a/solution.py
+++ b/solution.py
@@ -113,28 +113,35 @@
         return other, {"row": z * 2 + jnp.where(upper, 1, 0), "col": jnp.where(upper, other - C, other)}
 
     HALF, OWN = Z // 2, Z // 4
+    LAST = 3 if Z > 4 else 1
+    FIRST_LAST = OWN + HALF - LAST // 2
 
     def far_peer(i):
         step = jnp.where(i % 2 == 0, HALF + i // 2, HALF - i // 2)
         return wrap(OWN - step + Z, Z), {"row": wrap(z + step, Z) * 2 + core}
+
+    def lead_peer(i, to_core):
+        step = jnp.where(i % 2 == 0, HALF + i // 2, HALF - i // 2)
+        return {"row": wrap(z + step, Z) * 2 + to_core}
+
+    barrier = pltpu.get_barrier_semaphore()
+
+    def greet_far(i, carry):
+        pl.semaphore_signal(barrier, inc=1, device_id=far_peer(i)[1], device_id_type=MESH)
+        return carry
+
+    def greet_plane(i, carry):
+        pl.semaphore_signal(barrier, inc=1, device_id=plane_peer(i)[1], device_id_type=MESH)
+        return carry
+
+    lax.fori_loop(1, Z, greet_far, 0)
+
+    lax.fori_loop(1, D, greet_plane, 0)
 
     pairs = ((cur_hbm, cur), (res_hbm, res), (sha_hbm, sha), (site_hbm, site), (cls_hbm, cls), (pol_hbm, pol))
     loads = [pltpu.make_async_copy(a, b, in_sems.at[i]) for i, (a, b) in enumerate(pairs)]
     for load in loads:
         load.start()
-
-    barrier = pltpu.get_barrier_semaphore()
-
-    def greet_far(i, carry):
-        pl.semaphore_signal(barrier, inc=1, device_id=far_peer(i)[1], device_id_type=MESH)
-        return carry
-
-    def greet_plane(i, carry):
-        pl.semaphore_signal(barrier, inc=1, device_id=plane_peer(i)[1], device_id_type=MESH)
-        return carry
-
-    lax.fori_loop(1, Z, greet_far, 0)
-    lax.fori_loop(1, D, greet_plane, 0)
 
     wide[...] = jnp.zeros_like(wide)
     for load in loads:
@@ -212,13 +219,26 @@
     eight_group = lanes(8) // 16
     own_row = jnp.sum(jnp.where(eight_group == eight, stacked, 0.0), axis=0, keepdims=True)
 
+
     pl.semaphore_wait(barrier, Z + D - 2)
-    lax.fori_loop(1, D, send_here, 0)
-    lax.fori_loop(HALF + 1, Z, functools.partial(send_spot, 1), 0)
-    lax.fori_loop(1, HALF + 1, functools.partial(send_spot, 2), 0)
-    lax.fori_loop(1, HALF + 1, functools.partial(send_src, 3), 0)
-    lax.fori_loop(HALF + 1, Z, functools.partial(send_src, 4), 0)
-    lax.fori_loop(1, D, send_tgt, 0)
+    @pl.when(z < HALF)
+    def _():
+        lax.fori_loop(1, LAST + 1, functools.partial(send_spot, 2), 0, unroll=True)
+        lax.fori_loop(LAST + 1, HALF + 1, functools.partial(send_spot, 9), 0, unroll=True)
+        lax.fori_loop(1, HALF + 1, functools.partial(send_src, 3), 0, unroll=True)
+        lax.fori_loop(1, D, send_here, 0, unroll=True)
+        lax.fori_loop(HALF + 1, Z, functools.partial(send_spot, 1), 0, unroll=True)
+
+    @pl.when(z >= HALF)
+    def _():
+        lax.fori_loop(1, D, send_here, 0, unroll=True)
+        lax.fori_loop(HALF + 1, Z, functools.partial(send_spot, 1), 0, unroll=True)
+        lax.fori_loop(1, LAST + 1, functools.partial(send_spot, 2), 0, unroll=True)
+        lax.fori_loop(LAST + 1, HALF + 1, functools.partial(send_spot, 9), 0, unroll=True)
+        lax.fori_loop(1, HALF + 1, functools.partial(send_src, 3), 0, unroll=True)
+
+    lax.fori_loop(HALF + 1, Z, functools.partial(send_src, 4), 0, unroll=True)
+    lax.fori_loop(1, D, send_tgt, 0, unroll=True)
 
     drain(0, here_all, D - 1)
     for part in range(T // 128):
@@ -277,12 +297,16 @@
     drain(1, spot_all, Z - 1 - HALF)
     lax.fori_loop(0, HALF, spread_spots, 0, unroll=True)
     lax.fori_loop(0, HALF, fill, 0)
-    drain(2, spot_all, HALF)
-    lax.fori_loop(HALF, Z, spread_spots, 0, unroll=True)
-    lax.fori_loop(HALF, Z, fill, 0)
+    drain(9, spot_all, HALF - LAST)
+    for first, end in ((HALF, FIRST_LAST), (FIRST_LAST + LAST, Z)):
+        lax.fori_loop(first, end, spread_spots, 0, unroll=True)
+        lax.fori_loop(first, end, fill, 0)
     drain(4, src_all, Z - 1 - HALF)
     fields[0:PLANES, :] = jnp.concatenate(products(0), axis=0)
     fields[PLANES:128, :] = jnp.zeros((128 - PLANES, T), jnp.float32)
+    drain(2, spot_all, LAST)
+    lax.fori_loop(FIRST_LAST, FIRST_LAST + LAST, spread_spots, 0, unroll=True)
+    lax.fori_loop(FIRST_LAST, FIRST_LAST + LAST, fill, 0)
     drain(5, tgt_all, D - 1)
     tgt_t[...] = tgt_all[...].reshape(T, 128).T
     drain(3, src_all, HALF)
@@ -301,7 +325,7 @@
     den_all[q] = own_row - jnp.sum(jnp.where(diagonal, spread, 0.0), axis=0, keepdims=True)
 
     def send_den(i, carry):
-        copy(6, den_all.at[q], den_all.at[q], plane_peer(i)[1]).start()
+        copy(6, den_all.at[q], den_all.at[q], {"row": z * 2 + 1, "col": wrap(c + i, C)}).start()
         return carry
 
     def send_field(i, carry):
@@ -309,24 +333,51 @@
         copy(7, rs_send.at[other], rs_recv.at[q], device_id).start()
         return carry
 
-    def send_fin(i, carry):
-        slot, device_id = far_peer(i)
-        copy(8, fin_all.at[OWN], fin_all.at[slot], device_id).start()
-        return carry
-
-    lax.fori_loop(1, D, send_den, 0)
+    def send_fin(to_core, i, carry):
+        slot = far_peer(i)[0]
+        copy(8, fin_all.at[OWN], fin_all.at[slot], lead_peer(i, to_core)).start()
+        return carry
+
+    def of(which, buffer, count):
+        whole = buffer.at[pl.ds(0, count)]
+        return copy(which, whole, whole, far_peer(1)[1])
+
+    @pl.when(core == 0)
+    def _():
+        lax.fori_loop(0, C, send_den, 0)
+
+    @pl.when(core == 1)
+    def _():
+        lax.fori_loop(1, C, send_den, 0)
+
     rs_send[...] = fields[...].T.reshape(D, SH, 128)
     lax.fori_loop(1, D, send_field, 0)
     rs_recv[q] = rs_send[q]
-    drain(6, den_all, D - 1)
-    fin_all[OWN] = jnp.sum(den_all[...], axis=0)
-    lax.fori_loop(1, Z, send_fin, 0)
+
+    @pl.when(core == 1)
+    def _():
+        of(6, den_all, D - 1).wait_recv()
+        fin_all[OWN] = jnp.sum(den_all[...], axis=0)
+        lax.fori_loop(1, Z, functools.partial(send_fin, 1), 0)
+        lax.fori_loop(1, Z, functools.partial(send_fin, 0), 0)
+        copy(8, fin_all.at[OWN], fin_all.at[OWN], {"row": z * 2}).start()
+
     drain(7, rs_recv, D - 1)
     image = own - jnp.sum(rs_recv[...], axis=0)
     turned = swapped(image)
     img_out[...] = image[:, 0:PLANES]
 
-    drain(8, fin_all, Z - 1)
+    @pl.when(core == 0)
+    def _():
+        of(6, den_all, C).wait_send()
+        of(8, fin_all, Z).wait_recv()
+
+    @pl.when(core == 1)
+    def _():
+        of(6, den_all, C - 1).wait_send()
+        of(8, den_all, 2 * Z - 1).wait_send()
+        of(8, fin_all, Z - 1).wait_recv()
+
     ends = jnp.sum(fin_all[...], axis=0)
     ends = fold(jnp.where(eight_group == eight, ends, 0.0))
     den_re, den_im, rho_re, rho_im = (ends[i : i + 1] for i in range(4))
@@ -377,8 +428,8 @@
             pltpu.VMEM((D, 1, 128), f32),
             pltpu.VMEM((Z, 1, 128), f32),
             pltpu.SemaphoreType.DMA((6,)),
-            pltpu.SemaphoreType.DMA((9,)),
-            pltpu.SemaphoreType.DMA((9,)),
+            pltpu.SemaphoreType.DMA((10,)),
+            pltpu.SemaphoreType.DMA((10,)),
         ],
         compiler_params=pltpu.CompilerParams(
             collective_id=0, has_side_effects=True, vmem_limit_bytes=62 * 1024 * 1024

time: 41.4 us -> 41.6 us (level)
  no operation moved by 1% of the time
where the time goes in v4:
time: 41.6 us; the launch traced here: 41.4 us
  Pallas kernels  40.8 us (98%)
  between operations  0.64 us (2%)
    pallas_call x1, Pallas kernels, local(): pl.pallas_call(functools.partial(body, Z, C), out_shape=(pltpu.VMEM((SH,...  40.2 us

profile of v4, /device:TPU:1, one launch (start us, length us, event | category | flops | bytes accessed | tf_op | source)
XLA Modules:
  0.0 41.4 jit_solution(9632702662469328675)
XLA Ops:
  0.6 40.2 %shard_map.77 = (f32[16,96]{1,0:T(8,128)S(1)}, f32[16,96]{1,0:T(8,128)S(1)}) custom-call(f32[16,96]{1,0:T(8,128)} %bitcast.6, f32[16,96]{1,0:T(8,128)} %bitcast.7, f32[16,96]{1,0:T(8,128)} %bitcast.8, s32[3,16]{1,0:T(4,128)} %site_hbm.1, s32[1,16]{1,0:T(1,128)} %bitcast.9, f32[2,4]{1,0:T(2,128)} %pol_hbm.1), custom_call_target="tpu_custom_call" | custom-call | tf_op jit(solution)/shard_map/pallas_call | solution.py:403
  40.8 0.6 %shard_map.78 = (f32[16,96]{1,0:T(8,128)}, f32[16,96]{1,0:T(8,128)}) custom-call(f32[16,96]{1,0:T(8,128)S(1)} %get-tuple-element.6.image, f32[16,96]{1,0:T(8,128)S(1)} %get-tuple-element.7.half), custom_call_target="tpu_custom_call" | custom-call | tf_op jit(solution)/shard_map/pallas_call | solution.py:438

commit v5 on v4

--- a/solution.py
+++ b/solution.py
@@ -95,7 +95,7 @@
     cur_hbm, res_hbm, sha_hbm, site_hbm, cls_hbm, pol_hbm,
     img_out, half_out,
     cur, res, sha, site, cls, pol,
-    wide, src_all, spot_all, here_all, axes_t, axes_s, tgt_all, tgt_t, fields, ghi, glo, rs_send, rs_recv, den_all, fin_all,
+    wide, src_all, spot_all, here_all, axes_t, axes_s, tgt_all, tgt_t, fields, ghi, glo, rs_send, rs_recv, den_all, fin_all, every, total,
     in_sems, send_sems, recv_sems,
 ):
     r, c = lax.axis_index("row"), lax.axis_index("col")
@@ -333,15 +333,34 @@
         copy(7, rs_send.at[other], rs_recv.at[q], device_id).start()
         return carry
 
-    def send_fin(to_core, i, carry):
+    def send_fin(i, carry):
         slot = far_peer(i)[0]
-        copy(8, fin_all.at[OWN], fin_all.at[slot], lead_peer(i, to_core)).start()
+        peer = lead_peer(i, 1)
+        copy(8, fin_all.at[OWN], fin_all.at[slot], lead_peer(i, 0)).start()
+
+        @pl.when(jnp.logical_not((c == 0) & (peer["row"] == 1)))
+        def _():
+            copy(8, fin_all.at[OWN], fin_all.at[slot], peer).start()
+
         return carry
 
     def of(which, buffer, count):
         whole = buffer.at[pl.ds(0, count)]
         return copy(which, whole, whole, far_peer(1)[1])
 
+    COUNT = 2 * Z * C
+    first = (r == 1) & (c == 0)
+    others = jnp.logical_not(first)
+    me = r * C + c
+
+    @pl.when(others)
+    def _():
+        copy(10, den_all.at[q], every.at[me], {"row": 1, "col": 0}).start()
+
+    @pl.when(first)
+    def _():
+        every[me] = den_all[q]
+
     @pl.when(core == 0)
     def _():
         lax.fori_loop(0, C, send_den, 0)
@@ -358,8 +377,7 @@
     def _():
         of(6, den_all, D - 1).wait_recv()
         fin_all[OWN] = jnp.sum(den_all[...], axis=0)
-        lax.fori_loop(1, Z, functools.partial(send_fin, 1), 0)
-        lax.fori_loop(1, Z, functools.partial(send_fin, 0), 0)
+        lax.fori_loop(1, Z, send_fin, 0, unroll=True)
         copy(8, fin_all.at[OWN], fin_all.at[OWN], {"row": z * 2}).start()
 
     drain(7, rs_recv, D - 1)
@@ -367,18 +385,45 @@
     turned = swapped(image)
     img_out[...] = image[:, 0:PLANES]
 
+    @pl.when(first)
+    def _():
+        of(10, every, COUNT - 1).wait_recv()
+
+        def add(i, carry):
+            return carry + jnp.sum(every[pl.ds(i * SH, SH)], axis=0)
+
+        total[...] = lax.fori_loop(0, COUNT // SH, add, jnp.zeros((1, 128), jnp.float32), unroll=4)
+
+    @pl.when(others)
+    def _():
+        of(10, every, 1).wait_send()
+
     @pl.when(core == 0)
     def _():
         of(6, den_all, C).wait_send()
         of(8, fin_all, Z).wait_recv()
+        total[...] = jnp.sum(fin_all[...], axis=0)
 
     @pl.when(core == 1)
     def _():
         of(6, den_all, C - 1).wait_send()
+
+    skips = (core == 1) & (c == 0) & (z != 0)
+
+    @pl.when((core == 1) & jnp.logical_not(skips))
+    def _():
         of(8, den_all, 2 * Z - 1).wait_send()
+
+    @pl.when(skips)
+    def _():
+        of(8, den_all, 2 * Z - 2).wait_send()
+
+    @pl.when((core == 1) & others)
+    def _():
         of(8, fin_all, Z - 1).wait_recv()
-
-    ends = jnp.sum(fin_all[...], axis=0)
+        total[...] = jnp.sum(fin_all[...], axis=0)
+
+    ends = total[...]
     ends = fold(jnp.where(eight_group == eight, ends, 0.0))
     den_re, den_im, rho_re, rho_im = (ends[i : i + 1] for i in range(4))
     magnitude = jnp.maximum(den_re * den_re + den_im * den_im, 1.0)
@@ -427,9 +472,11 @@
             pltpu.VMEM((D, SH, 128), f32),
             pltpu.VMEM((D, 1, 128), f32),
             pltpu.VMEM((Z, 1, 128), f32),
+            pltpu.VMEM((R * C, 1, 128), f32),
+            pltpu.VMEM((1, 128), f32),
             pltpu.SemaphoreType.DMA((6,)),
-            pltpu.SemaphoreType.DMA((10,)),
-            pltpu.SemaphoreType.DMA((10,)),
+            pltpu.SemaphoreType.DMA((11,)),
+            pltpu.SemaphoreType.DMA((11,)),
         ],
         compiler_params=pltpu.CompilerParams(
             collective_id=0, has_side_effects=True, vmem_limit_bytes=62 * 1024 * 1024

time: 41.6 us -> 40.5 us (0.974)
  Pallas kernels: 40.8 us -> 39.7 us
    pallas_call x1, Pallas kernels: 40.2 us -> 39.1 us  [local(): pl.pallas_call(functools.partial(body, Z, C), out_shape=(pltpu.VMEM((SH,...]
where the time goes in v5:
time: 40.5 us; the launch traced here: 40.3 us
  Pallas kernels  39.7 us (98%)
  between operations  0.64 us (2%)
    pallas_call x1, Pallas kernels, local(): pl.pallas_call(functools.partial(body, Z, C), out_shape=(pltpu.VMEM((SH,...  39.1 us

profile of v5, /device:TPU:1, one launch (start us, length us, event | category | flops | bytes accessed | tf_op | source)
XLA Modules:
  0.0 40.3 jit_solution(18275065991766667472)
XLA Ops:
  0.6 39.1 %shard_map.77 = (f32[16,96]{1,0:T(8,128)S(1)}, f32[16,96]{1,0:T(8,128)S(1)}) custom-call(f32[16,96]{1,0:T(8,128)} %bitcast.6, f32[16,96]{1,0:T(8,128)} %bitcast.7, f32[16,96]{1,0:T(8,128)} %bitcast.8, s32[3,16]{1,0:T(4,128)} %site_hbm.1, s32[1,16]{1,0:T(1,128)} %bitcast.9, f32[2,4]{1,0:T(2,128)} %pol_hbm.1), custom_call_target="tpu_custom_call" | custom-call | tf_op jit(solution)/shard_map/pallas_call | solution.py:448
  39.7 0.6 %shard_map.78 = (f32[16,96]{1,0:T(8,128)}, f32[16,96]{1,0:T(8,128)}) custom-call(f32[16,96]{1,0:T(8,128)S(1)} %get-tuple-element.6.image, f32[16,96]{1,0:T(8,128)S(1)} %get-tuple-element.7.half), custom_call_target="tpu_custom_call" | custom-call | tf_op jit(solution)/shard_map/pallas_call | solution.py:485

commit v6 on v5

--- a/solution.py
+++ b/solution.py
@@ -88,6 +88,13 @@
     for shift in (64, 32, 16):
         block = block + pltpu.roll(block, shift, 1)
     return block
+
+
+def pairwise(stack):
+    while stack.shape[0] > 1:
+        half = stack.shape[0] // 2
+        stack = stack[:half] + stack[half:]
+    return stack[0]
 
 
 def body(
@@ -376,7 +383,7 @@
     @pl.when(core == 1)
     def _():
         of(6, den_all, D - 1).wait_recv()
-        fin_all[OWN] = jnp.sum(den_all[...], axis=0)
+        fin_all[OWN] = pairwise(den_all[...])
         lax.fori_loop(1, Z, send_fin, 0, unroll=True)
         copy(8, fin_all.at[OWN], fin_all.at[OWN], {"row": z * 2}).start()
 
@@ -390,9 +397,10 @@
         of(10, every, COUNT - 1).wait_recv()
 
         def add(i, carry):
-            return carry + jnp.sum(every[pl.ds(i * SH, SH)], axis=0)
-
-        total[...] = lax.fori_loop(0, COUNT // SH, add, jnp.zeros((1, 128), jnp.float32), unroll=4)
+            return carry + every[pl.ds(i * SH, SH)]
+
+        sixteen = lax.fori_loop(1, COUNT // SH, add, every[0:SH], unroll=True)
+        total[...] = pairwise(sixteen)
 
     @pl.when(others)
     def _():
@@ -402,7 +410,7 @@
     def _():
         of(6, den_all, C).wait_send()
         of(8, fin_all, Z).wait_recv()
-        total[...] = jnp.sum(fin_all[...], axis=0)
+        total[...] = pairwise(fin_all[...])
 
     @pl.when(core == 1)
     def _():
@@ -421,7 +429,7 @@
     @pl.when((core == 1) & others)
     def _():
         of(8, fin_all, Z - 1).wait_recv()
-        total[...] = jnp.sum(fin_all[...], axis=0)
+        total[...] = pairwise(fin_all[...])
 
     ends = total[...]
     ends = fold(jnp.where(eight_group == eight, ends, 0.0))

time: 40.5 us -> 40.4 us (level)
  no operation moved by 1% of the time
where the time goes in v6:
time: 40.4 us; the launch traced here: 40.2 us
  Pallas kernels  39.5 us (98%)
  between operations  0.64 us (2%)
    pallas_call x1, Pallas kernels, local(): pl.pallas_call(functools.partial(body, Z, C), out_shape=(pltpu.VMEM((SH,...  38.9 us

profile of v6, /device:TPU:1, one launch (start us, length us, event | category | flops | bytes accessed | tf_op | source)
XLA Modules:
  0.0 40.2 jit_solution(17244897942730605262)
XLA Ops:
  0.6 38.9 %shard_map.77 = (f32[16,96]{1,0:T(8,128)S(1)}, f32[16,96]{1,0:T(8,128)S(1)}) custom-call(f32[16,96]{1,0:T(8,128)} %bitcast.6, f32[16,96]{1,0:T(8,128)} %bitcast.7, f32[16,96]{1,0:T(8,128)} %bitcast.8, s32[3,16]{1,0:T(4,128)} %site_hbm.1, s32[1,16]{1,0:T(1,128)} %bitcast.9, f32[2,4]{1,0:T(2,128)} %pol_hbm.1), custom_call_target="tpu_custom_call" | custom-call | tf_op jit(solution)/shard_map/pallas_call | solution.py:456
  39.6 0.6 %shard_map.78 = (f32[16,96]{1,0:T(8,128)}, f32[16,96]{1,0:T(8,128)}) custom-call(f32[16,96]{1,0:T(8,128)S(1)} %get-tuple-element.6.image, f32[16,96]{1,0:T(8,128)S(1)} %get-tuple-element.7.half), custom_call_target="tpu_custom_call" | custom-call | tf_op jit(solution)/shard_map/pallas_call | solution.py:493

commit v7 on v6

--- a/solution.py
+++ b/solution.py
@@ -102,7 +102,7 @@
     cur_hbm, res_hbm, sha_hbm, site_hbm, cls_hbm, pol_hbm,
     img_out, half_out,
     cur, res, sha, site, cls, pol,
-    wide, src_all, spot_all, here_all, axes_t, axes_s, tgt_all, tgt_t, fields, ghi, glo, rs_send, rs_recv, den_all, fin_all, every, total,
+    wide, src_all, spot_all, here_all, axes_t, axes_s, tgt_all, tgt_t, fields, ghi, glo, rs_send, rs_recv, den_all, fin_all, every, total, den_near,
     in_sems, send_sems, recv_sems,
 ):
     r, c = lax.axis_index("row"), lax.axis_index("col")
@@ -316,16 +316,20 @@
     lax.fori_loop(FIRST_LAST, FIRST_LAST + LAST, fill, 0)
     drain(5, tgt_all, D - 1)
     tgt_t[...] = tgt_all[...].reshape(T, 128).T
-    drain(3, src_all, HALF)
-    parts = products(1)
     den_re = den_im = 0.0
     for i in range(3):
         sr, si = rows(tgt_t, 0, i), rows(tgt_t, 1, i)
-        re, im = rows(fields, 0, i) + parts[i], rows(fields, 1, i) + parts[3 + i]
+        re, im = rows(fields, 0, i), rows(fields, 1, i)
         den_re = den_re + sr * re + si * im
         den_im = den_im + sr * im - si * re
-        fields[i * 16 : i * 16 + 16, :] = re
-        fields[48 + i * 16 : 64 + i * 16, :] = im
+    den_near[0], den_near[1] = den_re, den_im
+    drain(3, src_all, HALF)
+    den_re, den_im = den_near[0], den_near[1]
+    parts = products(1)
+    for i in range(3):
+        sr, si = rows(tgt_t, 0, i), rows(tgt_t, 1, i)
+        den_re = den_re + sr * parts[i] + si * parts[3 + i]
+        den_im = den_im + sr * parts[3 + i] - si * parts[i]
     den_re = jnp.sum(den_re, axis=1, keepdims=True)
     den_im = jnp.sum(den_im, axis=1, keepdims=True)
     spread = jnp.where(group == 0, den_re, jnp.where(group == 1, den_im, 0.0))
@@ -370,12 +374,13 @@
 
     @pl.when(core == 0)
     def _():
-        lax.fori_loop(0, C, send_den, 0)
+        lax.fori_loop(0, C, send_den, 0, unroll=True)
 
     @pl.when(core == 1)
     def _():
-        lax.fori_loop(1, C, send_den, 0)
-
+        lax.fori_loop(1, C, send_den, 0, unroll=True)
+
+    fields[0:PLANES, :] += jnp.concatenate(parts, axis=0)
     rs_send[...] = fields[...].T.reshape(D, SH, 128)
     lax.fori_loop(1, D, send_field, 0)
     rs_recv[q] = rs_send[q]
@@ -482,6 +487,7 @@
             pltpu.VMEM((Z, 1, 128), f32),
             pltpu.VMEM((R * C, 1, 128), f32),
             pltpu.VMEM((1, 128), f32),
+            pltpu.VMEM((2, SH, T), f32),
             pltpu.SemaphoreType.DMA((6,)),
             pltpu.SemaphoreType.DMA((11,)),
             pltpu.SemaphoreType.DMA((11,)),

time: 40.4 us -> 40.4 us (level)
  no operation moved by 1% of the time
where the time goes in v7:
time: 40.4 us; the launch traced here: 40.2 us
  Pallas kernels  39.6 us (98%)
  between operations  0.64 us (2%)
    pallas_call x1, Pallas kernels, local(): pl.pallas_call(functools.partial(body, Z, C), out_shape=(pltpu.VMEM((SH,...  38.9 us

profile of v7, /device:TPU:1, one launch (start us, length us, event | category | flops | bytes accessed | tf_op | source)
XLA Modules:
  0.0 40.2 jit_solution(14300887362902332988)
XLA Ops:
  0.6 38.9 %shard_map.77 = (f32[16,96]{1,0:T(8,128)S(1)}, f32[16,96]{1,0:T(8,128)S(1)}) custom-call(f32[16,96]{1,0:T(8,128)} %bitcast.6, f32[16,96]{1,0:T(8,128)} %bitcast.7, f32[16,96]{1,0:T(8,128)} %bitcast.8, s32[3,16]{1,0:T(4,128)} %site_hbm.1, s32[1,16]{1,0:T(1,128)} %bitcast.9, f32[2,4]{1,0:T(2,128)} %pol_hbm.1), custom_call_target="tpu_custom_call" | custom-call | tf_op jit(solution)/shard_map/pallas_call | solution.py:461
  39.6 0.6 %shard_map.78 = (f32[16,96]{1,0:T(8,128)}, f32[16,96]{1,0:T(8,128)}) custom-call(f32[16,96]{1,0:T(8,128)S(1)} %get-tuple-element.6.image, f32[16,96]{1,0:T(8,128)S(1)} %get-tuple-element.7.half), custom_call_target="tpu_custom_call" | custom-call | tf_op jit(solution)/shard_map/pallas_call | solution.py:499

commit v8 on v6

--- a/solution.py
+++ b/solution.py
@@ -370,11 +370,11 @@
 
     @pl.when(core == 0)
     def _():
-        lax.fori_loop(0, C, send_den, 0)
+        lax.fori_loop(0, C, send_den, 0, unroll=True)
 
     @pl.when(core == 1)
     def _():
-        lax.fori_loop(1, C, send_den, 0)
+        lax.fori_loop(1, C, send_den, 0, unroll=True)
 
     rs_send[...] = fields[...].T.reshape(D, SH, 128)
     lax.fori_loop(1, D, send_field, 0)

time: 40.4 us -> 40.4 us (level)
  no operation moved by 1% of the time
where the time goes in v8:
time: 40.4 us; the launch traced here: 40.2 us
  Pallas kernels  39.5 us (98%)
  between operations  0.64 us (2%)
    pallas_call x1, Pallas kernels, local(): pl.pallas_call(functools.partial(body, Z, C), out_shape=(pltpu.VMEM((SH,...  38.9 us

profile of v8, /device:TPU:1, one launch (start us, length us, event | category | flops | bytes accessed | tf_op | source)
XLA Modules:
  0.0 40.2 jit_solution(12634332877072174770)
XLA Ops:
  0.6 38.9 %shard_map.77 = (f32[16,96]{1,0:T(8,128)S(1)}, f32[16,96]{1,0:T(8,128)S(1)}) custom-call(f32[16,96]{1,0:T(8,128)} %bitcast.6, f32[16,96]{1,0:T(8,128)} %bitcast.7, f32[16,96]{1,0:T(8,128)} %bitcast.8, s32[3,16]{1,0:T(4,128)} %site_hbm.1, s32[1,16]{1,0:T(1,128)} %bitcast.9, f32[2,4]{1,0:T(2,128)} %pol_hbm.1), custom_call_target="tpu_custom_call" | custom-call | tf_op jit(solution)/shard_map/pallas_call | solution.py:456
  39.6 0.6 %shard_map.78 = (f32[16,96]{1,0:T(8,128)}, f32[16,96]{1,0:T(8,128)}) custom-call(f32[16,96]{1,0:T(8,128)S(1)} %get-tuple-element.6.image, f32[16,96]{1,0:T(8,128)S(1)} %get-tuple-element.7.half), custom_call_target="tpu_custom_call" | custom-call | tf_op jit(solution)/shard_map/pallas_call | solution.py:493
